TPU v7x, 32 devices: a whole 2x2x4 slice. The times are simulated.
32 devices in a mesh: groups: 2 (over x), slab: 16 (over z, y, core).
Axes of the slice: x: 2, y: 2, z: 4, core: 2. Of those that a mesh axis runs over, the one named last changes fastest.
Arguments:
- latent: bfloat16 [64, 32, 2048], P(None, ('groups', 'slab')), parts along dimension 1, may hold values from -6 to 6
- conv1_weight: bfloat16 [27, 64, 64], replicated, may hold values from -0.15625 to 0.15625
- conv2_weight: bfloat16 [27, 64, 64], replicated, may hold values from -0.15625 to 0.15625
- head: bfloat16 [64], replicated, may hold values from -2 to 2
- p_prev: float32 [32, 16, 64, 128], P(('groups', 'slab')), parts along dimension 0, may hold values from -6 to 6
- p_cur: float32 [32, 16, 64, 128], P(('groups', 'slab')), parts along dimension 0, may hold values from -6 to 6
- adjoint: bfloat16 [4, 32, 16, 64, 128], P(None, ('groups', 'slab')), parts along dimension 1, may hold values from -6 to 6
- wavelet: float32 [16, 4], P('groups'), parts along dimension 0, may hold values from -12 to 12
- sources: int32 [16, 3], P('groups'), parts along dimension 0, may hold values from 0 to 127, as said below
- receivers: int32 [16, 3, 128], P('groups'), parts along dimension 0, may hold values from 0 to 127, as said below
Outputs:
- pressure_final: float32 [32, 16, 64, 128], P(('groups', 'slab')), parts along dimension 0
- traces: float32 [16, 4, 128], P('groups'), parts along dimension 0
- gradient: float32 [32, 2048], P(('groups', 'slab')), parts along dimension 0
There are 2 independent parts, one for each index of `groups`. A program takes and returns all parts, laid end to end along the dimension named above; an argument that names none is the same for every part. Nothing has to cross between parts.
Inputs may be any that keep to these rules, and one draw needn't show every extreme that they name: sources[s] is the source cell (depth, row, column) of shot s on the fine grid: depth below 32, row below 64, column below 128. receivers[s, :, k] is the cell (depth, row, column) of receiver k of shot s on the fine grid: depth below 32, row below 64, column below 128.
All inputs are finite; a program needn't handle non-finite values.
Results may differ from a plain program's by a relative error of at most 0.006.
Values may be sent and summed in bfloat16 or wider, within the bound.
A program may use at most 64 MiB of HBM per device.

v0:
```python
import jax
import jax.numpy as jnp
from jax import lax
from jax.sharding import PartitionSpec as P

CY = 32
CX = 64
SHOTS = 8
STEPS = 4
stencil_weights = (-205.0 / 72.0, 8.0 / 5.0, -1.0 / 5.0, 8.0 / 315.0, -1.0 / 560.0)
lowest_speed = 1.5
speed_range = 3.0
courant = 0.088
leak_slope = 0.2


def extended_2(block, sides, width):
    for axis, dim in sides:
        count = lax.axis_size(axis)
        forward = [(i, i + 1) for i in range(count - 1)]
        backward = [(target, source) for source, target in forward]
        low = lax.ppermute(
            lax.slice_in_dim(block, block.shape[dim] - width, None, axis=dim), axis, forward
        )
        high = lax.ppermute(lax.slice_in_dim(block, 0, width, axis=dim), axis, backward)
        block = jnp.concatenate([low, block, high], axis=dim)
    return block


def from_partner(value, axis, apart):
    mask = 2**apart
    pairs = [(source, source ^ mask) for source in range(lax.axis_size(axis))]
    return lax.ppermute(value, axis, pairs)


def for_sending(shard):
    return jax.tree.map(lambda a: a.astype(jnp.bfloat16) if a.dtype == jnp.float32 else a, shard)


def from_behind(value, axis, steps):
    count = lax.axis_size(axis)
    leading, last = (max(0, -steps), min(count, count - steps))
    return lax.ppermute(value, axis, [(source, source + steps) for source in range(leading, last)])


def conv_taps(extended_in, weight):
    planes = extended_in.shape[1] - 2
    cell_count = extended_in.shape[2]
    extended = jnp.pad(extended_in, ((0, 0), (0, 0), (CX + 1, CX + 1)))
    columns = jnp.arange(cell_count) % CX
    accumulated = jnp.zeros((weight.shape[1], planes, cell_count), jnp.float32)
    tap_index = 0
    for depth_off in range(3):
        for row_off in (-1, 0, 1):
            for col_off in (-1, 0, 1):
                begin_at = CX + 1 + row_off * CX + col_off
                piece = extended[
                    :, depth_off : depth_off + planes, begin_at : begin_at + cell_count
                ]
                column_valid = ((columns + col_off >= 0) & (columns + col_off < CX)).astype(
                    extended.dtype
                )
                accumulated = accumulated + jnp.einsum(
                    "oi,izn->ozn",
                    weight[tap_index],
                    piece * column_valid,
                    preferred_element_type=jnp.float32,
                )
                tap_index += 1
    return accumulated


def double_axis(values, axis):
    length = values.shape[axis]
    lower_side = jnp.concatenate(
        [
            lax.slice_in_dim(values, 0, 1, axis=axis),
            lax.slice_in_dim(values, 0, length - 1, axis=axis),
        ],
        axis=axis,
    )
    upper_side = jnp.concatenate(
        [
            lax.slice_in_dim(values, 1, length, axis=axis),
            lax.slice_in_dim(values, length - 1, length, axis=axis),
        ],
        axis=axis,
    )
    even_part = 0.75 * values + 0.25 * lower_side
    odd_part = 0.75 * values + 0.25 * upper_side
    new_shape = list(values.shape)
    new_shape[axis] = 2 * length
    return jnp.stack([even_part, odd_part], axis=axis + 1).reshape(new_shape)


def double_depth(rimmed):
    inner_planes = rimmed.shape[0] - 2
    middle = rimmed[1:-1]
    even_part = 0.75 * middle + 0.25 * rimmed[:-2]
    odd_part = 0.75 * middle + 0.25 * rimmed[2:]
    return jnp.stack([even_part, odd_part], axis=1).reshape((2 * inner_planes,) + rimmed.shape[1:])


def upsample_slab(rimmed):
    deeper = double_depth(rimmed).reshape(2 * (rimmed.shape[0] - 2), CY, CX)
    return double_axis(double_axis(deeper, 1), 2)


def stencil(extended):
    depth_total = extended.shape[0] - 8
    row_total = extended.shape[1]
    col_total = extended.shape[2]
    padded = jnp.pad(extended, ((0, 0), (4, 4), (4, 4)))

    def window(depth_at, row_at, col_at):
        return padded[
            depth_at : depth_at + depth_total,
            row_at : row_at + row_total,
            col_at : col_at + col_total,
        ]

    accumulated = 3.0 * stencil_weights[0] * window(4, 4, 4)
    for reach in range(1, 5):
        near_sum = window(4 - reach, 4, 4) + window(4 + reach, 4, 4)
        near_sum = near_sum + window(4, 4 - reach, 4) + window(4, 4 + reach, 4)
        near_sum = near_sum + window(4, 4, 4 - reach) + window(4, 4, 4 + reach)
        accumulated = accumulated + stencil_weights[reach] * near_sum
    return accumulated


def body(
    latent, conv1_weight, conv2_weight, head, p_prev, p_cur, adjoint, wavelet, sources, receivers
):
    position = lax.axis_index("slab")
    devices = lax.axis_size("slab")
    my_shot = position % SHOTS
    slab_index = position // SHOTS
    slab_total = devices // SHOTS
    group_bits = SHOTS.bit_length() - 1
    latent_wide = extended_2(latent, (("slab", 1),), 1)
    hidden = jax.nn.leaky_relu(conv_taps(latent_wide, conv1_weight), leak_slope).astype(
        jnp.bfloat16
    )
    hidden_wide = extended_2(hidden, (("slab", 1),), 1)
    second = jax.nn.leaky_relu(conv_taps(hidden_wide, conv2_weight), leak_slope)
    logits = jnp.einsum(
        "c,czn->zn", head.astype(jnp.float32), second, precision=lax.Precision.HIGHEST
    )
    velocity = (lowest_speed + speed_range * jax.nn.sigmoid(logits)).astype(jnp.bfloat16)
    planes = velocity.shape[0]
    slab_planes = planes * SHOTS
    rimmed = extended_2(velocity, (("slab", 0),), 1)
    rimmed = jnp.concatenate(
        [
            jnp.where(position == 0, velocity, rimmed[:1]),
            rimmed[1:-1],
            jnp.where(position == devices - 1, velocity, rimmed[-1:]),
        ],
        axis=0,
    )
    tile_doubled = double_depth(rimmed.astype(jnp.float32))
    bit_order = list(range(group_bits))
    blocks = tile_doubled[None]
    for bit_index in bit_order:
        partner = from_partner(blocks, "slab", bit_index)
        upper_bit = my_shot // (1 << bit_index) % 2 == 1
        blocks = jnp.where(
            upper_bit,
            jnp.concatenate([partner, blocks], axis=0),
            jnp.concatenate([blocks, partner], axis=0),
        )
    placed = []
    for shot_number in range(SHOTS):
        list_index = 0
        for section_number in range(group_bits):
            list_index = list_index + (
                (shot_number >> bit_order[section_number] & 1) << section_number
            )
        placed.append(blocks[list_index])
    deeper = jnp.concatenate(placed, axis=0).reshape(2 * slab_planes, CY, CX)
    fine_speed = double_axis(double_axis(deeper, 1), 2)
    courant_sq = (courant * fine_speed) ** 2
    previous = p_prev[0]
    current = p_cur[0]
    fine_planes = current.shape[0]
    offset = slab_index * fine_planes
    source = lax.dynamic_index_in_dim(sources, my_shot, 0, keepdims=False)
    station = lax.dynamic_index_in_dim(receivers, my_shot, 0, keepdims=False)
    pulses = lax.dynamic_index_in_dim(wavelet, my_shot, 0, keepdims=False)
    source_depth = source[0] - offset
    source_inside = (source_depth >= 0) & (source_depth < fine_planes)
    source_depth = jnp.clip(source_depth, 0, fine_planes - 1)
    station_depth = station[0] - offset
    station_inside = (station_depth >= 0) & (station_depth < fine_planes)
    station_depth = jnp.clip(station_depth, 0, fine_planes - 1)
    correlation = jnp.zeros(current.shape, jnp.float32)
    samples_list = []
    for step_index in range(STEPS):
        rim_below = from_behind(for_sending(current[-4:]), "slab", SHOTS)
        rim_above = from_behind(for_sending(current[:4]), "slab", -SHOTS)
        laplace_term = stencil(jnp.concatenate([rim_below, current, rim_above], axis=0))
        correlation = correlation + adjoint[step_index, 0].astype(jnp.float32) * laplace_term
        advanced = 2.0 * current - previous + courant_sq * laplace_term
        advanced = advanced.at[source_depth, source[1], source[2]].add(
            jnp.where(source_inside, pulses[step_index], 0.0)
        )
        samples_list.append(
            jnp.where(station_inside, advanced[station_depth, station[1], station[2]], 0.0)
        )
        previous, current = (current, advanced)
    record = jnp.stack(samples_list)
    own_traces = jnp.where((jnp.arange(SHOTS) == my_shot)[:, None, None], record[None], 0.0)
    traces = lax.psum(own_traces, "slab")
    fine_gradient = 2.0 * courant * courant * fine_speed * correlation
    shape_holder = jnp.zeros((slab_planes + 2, velocity.shape[1]), jnp.float32)
    unused, pullback = jax.vjp(upsample_slab, shape_holder)
    grad_rim = pullback(fine_gradient)[0]
    first_slab = slab_index == 0
    last_slab = slab_index == slab_total - 1
    folded = jnp.concatenate(
        [
            jnp.where(first_slab, 0.0, grad_rim[:1]),
            grad_rim[1:2] + jnp.where(first_slab, grad_rim[:1], 0.0),
            grad_rim[2:-2],
            grad_rim[-2:-1] + jnp.where(last_slab, grad_rim[-1:], 0.0),
            jnp.where(last_slab, 0.0, grad_rim[-1:]),
        ],
        axis=0,
    )
    from_lower = from_behind(folded[-1:], "slab", SHOTS)
    from_upper = from_behind(folded[:1], "slab", -SHOTS)
    inner = folded[1:-1]
    inner = jnp.concatenate([inner[:1] + from_lower, inner[1:-1], inner[-1:] + from_upper], axis=0)
    blocks = inner.reshape(SHOTS, planes, inner.shape[1])
    for bit_index in reversed(range(group_bits)):
        halfway = blocks.shape[0] // 2
        upper_bit = my_shot // (1 << bit_index) % 2 == 1
        retained = jnp.where(upper_bit, blocks[halfway:], blocks[:halfway])
        outgoing = jnp.where(upper_bit, blocks[:halfway], blocks[halfway:])
        blocks = retained + from_partner(outgoing, "slab", bit_index)
    gradient = blocks[0]
    return (current[None], traces, gradient)


def solution(mesh):
    in_specs = (
        P(None, ("groups", "slab"), None),
        P(),
        P(),
        P(),
        P(("groups", "slab"), None, None, None),
        P(("groups", "slab"), None, None, None),
        P(None, ("groups", "slab"), None, None, None),
        P("groups", None),
        P("groups", None),
        P("groups", None, None),
    )
    out_specs = (
        P(("groups", "slab"), None, None, None),
        P("groups", None, None),
        P(("groups", "slab"), None),
    )
    return jax.shard_map(body, mesh=mesh, in_specs=in_specs, out_specs=out_specs, check_vma=False)
```

profile of v0, /device:TPU:0, one launch (start us, length us, event | category | flops | bytes accessed | tf_op | source)
XLA Modules:
  0.0 228.8 jit_solution(11264955654170186735)
XLA Ops:
  2.1 3.1 %collective-permute-start = (bf16[64,1,2048]{2,0,1:T(8,128)(2,1)}, bf16[64,1,2048]{2,0,1:T(8,128)(2,1)S(1)}, u32[]{:S(2)}, u32[]{:S(2)}) collective-permute-start(bf16[64,1,2048]{2,0,1:T(8,128)(2,1)} %param.18), channel_id=1, source_target_pairs={{0,1},{1,2},{2,3},{3,4},{4,5},{5,6},{6,7},{7,8},{8,9},{9,10},{10,1... | collective-permute-start | bytes 786440 | tf_op jit(solution)/shard_map/ppermute | solution.py:22
  16.5 9.2 %collective-permute-start.2 = (bf16[64,1,2048]{2,0,1:T(8,128)(2,1)S(1)}, bf16[64,1,2048]{2,0,1:T(8,128)(2,1)S(1)}, u32[]{:S(2)}, u32[]{:S(2)}) collective-permute-start(bf16[64,1,2048]{2,0,1:T(8,128)(2,1)S(1)} %bitcast.577), channel_id=1, source_target_pairs={{0,1},{1,2},{2,3},{3,4},{4,5},{5,6},{6,7},{7,8},{8,9},{9,10},{10,1... | collective-permute-start | bytes 786440 | tf_op jit(solution)/shard_map/ppermute | solution.py:22
  25.7 5.7 %collective-permute-start.9 = (bf16[4,64,128]{2,1,0:T(8,128)(2,1)S(1)}, bf16[4,64,128]{2,1,0:T(8,128)(2,1)S(1)}, u32[]{:S(2)}, u32[]{:S(2)}) collective-permute-start(bf16[4,64,128]{2,1,0:T(8,128)(2,1)S(1)} %get-tuple-element.81), channel_id=1, source_target_pairs={{0,8},{1,9},{2,10},{3,11},{4,12},{5,13},{6,14},{7,15},{16,24},{17,... | collective-permute-start | bytes 196616 | tf_op jit(solution)/shard_map/ppermute | solution.py:43
  42.9 3.6 %collective-permute-start.4 = (bf16[1,2048]{1,0:T(2,128)(2,1)S(1)}, bf16[1,2048]{1,0:T(2,128)(2,1)S(1)}, u32[]{:S(2)}, u32[]{:S(2)}) collective-permute-start(bf16[1,2048]{1,0:T(2,128)(2,1)S(1)} %convert_element_type.266), channel_id=1, source_target_pairs={{0,1},{1,2},{2,3},{3,4},{4,5},{5,6},{6,7},{7,8},{8,9},{9,10},{10,1... | collective-permute-start | bytes 12296 | tf_op jit(solution)/shard_map/ppermute | solution.py:22
  47.4 1.8 collective-permute-start.6
  54.2 2.4 %collective-permute-start.7 = (f32[2,2,2048]{2,1,0:T(2,128)S(1)}, f32[2,2,2048]{2,1,0:T(2,128)S(1)}, u32[]{:S(2)}, u32[]{:S(2)}) collective-permute-start(f32[2,2,2048]{2,1,0:T(2,128)S(1)} %maximum_select_fusion.2), channel_id=1, source_target_pairs={{0,2},{1,3},{2,0},{3,1},{4,6},{5,7},{6,4},{7,5},{8,10},{9,11},{10,... | collective-permute-start | bytes 98312 | tf_op jit(solution)/shard_map/ppermute | solution.py:33
  60.1 2.2 collective-permute-start.8
  62.8 1.7 collective-permute-done.8
  72.2 1.7 fusion.155
  75.1 1.9 copy.58
  77.0 1.6 copy.59
  78.6 4.4 %fusion.164 = (f32[16,64,128]{2,1,0:T(8,128)S(1)}, f32[16,64,128]{2,1,0:T(8,128)}) fusion(f32[1,16,64,128]{3,2,1,0:T(8,128)} %param.22, f32[16,64,128]{2,1,0:T(8,128)S(1)} %copy.59, f32[1,16,64,128]{3,2,1,0:T(8,128)S(1)} %copy-done.2, f32[24,72,136]{2,1,0:T(8,128)S(1)} %select_maximum_fusion.6, f32[4,64,128]{2,1,0:T(8,128)} %copy-done.11, ...), kind=kLoop, calls=%fused_computation.321 | loop fusion | flops 5373952 | bytes 11796480 | tf_op jit(solution)/shard_map/add | solution.py:203
  85.7 5.2 %collective-permute-start.11 = (bf16[4,64,128]{2,1,0:T(8,128)(2,1)S(1)}, bf16[4,64,128]{2,1,0:T(8,128)(2,1)S(1)}, u32[]{:S(2)}, u32[]{:S(2)}) collective-permute-start(bf16[4,64,128]{2,1,0:T(8,128)(2,1)S(1)} %get-tuple-element.79), channel_id=1, source_target_pairs={{0,8},{1,9},{2,10},{3,11},{4,12},{5,13},{6,14},{7,15},{16,24},{17,... | collective-permute-start | bytes 196616 | tf_op jit(solution)/shard_map/ppermute | solution.py:43
  92.7 5.2 %collective-permute-done.12 = bf16[4,64,128]{2,1,0:T(8,128)(2,1)S(1)} collective-permute-done((bf16[4,64,128]{2,1,0:T(8,128)(2,1)S(1)}, bf16[4,64,128]{2,1,0:T(8,128)(2,1)S(1)}, u32[]{:S(2)}, u32[]{:S(2)}) %collective-permute-start.12) | collective-permute-done | bytes 65568 | tf_op jit(solution)/shard_map/ppermute | solution.py:43
  99.1 4.2 %multiply_add_fusion.2 = (f32[16,64,128]{2,1,0:T(8,128)S(1)}, f32[16,64,128]{2,1,0:T(8,128)}) fusion(f32[16,64,128]{2,1,0:T(8,128)} %copy-done.3, f32[16,64,128]{2,1,0:T(8,128)S(1)} %scatter-add.14, f32[1,16,64,128]{3,2,1,0:T(8,128)S(1)} %copy-done.2, f32[24,72,136]{2,1,0:T(8,128)S(1)} %select_maximum_fusion.4, f32[4,64,128]{2,1,0:T(8,128)} %copy-done.13, ...), kind=kLoop, calls=%fused_computation.326 | loop fusion | flops 5373952 | bytes 11272192 | tf_op jit(solution)/shard_map/add | solution.py:203
  106.1 1.6 collective-permute-start.13
  107.7 1.5 collective-permute-start.14
  110.0 1.5 gather_fusion
  111.5 3.3 %collective-permute-done.14 = bf16[4,64,128]{2,1,0:T(8,128)(2,1)S(1)} collective-permute-done((bf16[4,64,128]{2,1,0:T(8,128)(2,1)S(1)}, bf16[4,64,128]{2,1,0:T(8,128)(2,1)S(1)}, u32[]{:S(2)}, u32[]{:S(2)}) %collective-permute-start.14) | collective-permute-done | bytes 65568 | tf_op jit(solution)/shard_map/ppermute | solution.py:43
  116.0 4.2 %multiply_add_fusion.1 = (f32[16,64,128]{2,1,0:T(8,128)S(1)}, f32[16,64,128]{2,1,0:T(8,128)}) fusion(f32[16,64,128]{2,1,0:T(8,128)} %copy-done.3, f32[16,64,128]{2,1,0:T(8,128)S(1)} %scatter-add.14, f32[16,64,128]{2,1,0:T(8,128)S(1)} %scatter-add.15, f32[24,72,136]{2,1,0:T(8,128)S(1)} %select_maximum_fusion.2, f32[4,64,128]{2,1,0:T(8,128)} %copy-done.12, ...), kind=kLoop, calls=%fused_computation.325 | loop fusion | flops 5373952 | bytes 11272192 | tf_op jit(solution)/shard_map/add | solution.py:203
  123.0 2.2 collective-permute-start.15
  127.2 2.0 copy.63
  129.2 2.4 %copy.64 = f32[16,64,128]{2,1,0:T(8,128)} copy(f32[16,64,128]{1,0,2:T(8,128)} %bitcast.569) | data formatting | bytes 1048576 | tf_op jit(solution)/shard_map/mul | solution.py:214
  136.0 3.4 %fusion.158 = (f32[16,64,128]{2,1,0:T(8,128)}, f32[16,64,128]{2,1,0:T(8,128)S(1)}) fusion(f32[16,64,128]{2,1,0:T(8,128)S(1)} %copy-done.10, f32[16,64,128]{2,1,0:T(8,128)S(1)} %copy-done.9, f32[16,64,128]{2,1,0:T(8,128)S(1)} %copy-done.8, f32[16,64,128]{2,1,0:T(8,128)S(1)} %copy-done.7, bf16[4,1,16,64,128]{4,3,2,1,0:T(8,128)(2,1)S(1)} %copy-done.14, ...), kind=kLoop, calls=%fused_computation.310 | loop fusion | flops 6422528 | bytes 13369344 | tf_op jit(solution)/shard_map/mul | solution.py:214
  143.7 1.5 copy.65
  148.5 5.4 %collective-permute-start.18 = (f32[1,2048]{1,0:T(1,128)S(1)}, f32[1,2048]{1,0:T(1,128)S(1)}, u32[]{:S(2)}, u32[]{:S(2)}) collective-permute-start(f32[1,2048]{1,0:T(1,128)S(1)} %get-tuple-element.91), channel_id=1, source_target_pairs={{0,8},{1,9},{2,10},{3,11},{4,12},{5,13},{6,14},{7,15},{16,24},{17,... | collective-permute-start | bytes 24584 | tf_op jit(solution)/shard_map/ppermute | solution.py:43
  155.3 5.1 %collective-permute-done.17 = f32[1,2048]{1,0:T(1,128)S(1)} collective-permute-done((f32[1,2048]{1,0:T(1,128)S(1)}, f32[1,2048]{1,0:T(1,128)S(1)}, u32[]{:S(2)}, u32[]{:S(2)}) %collective-permute-start.17) | collective-permute-done | bytes 8224 | tf_op jit(solution)/shard_map/ppermute | solution.py:43
  160.5 2.1 collective-permute-start.19
  162.6 1.9 collective-permute-done.19
  164.5 1.8 collective-permute-start.20
  166.4 2.0 collective-permute-done.20
  168.4 59.7 %psum.7 = f32[8,4,128]{2,1,0:T(4,128)} all-reduce(f32[8,4,128]{2,1,0:T(4,128)S(1)} %broadcast_select_fusion.9), channel_id=1, replica_groups=mesh['groups'=2,'slab'=16] {'slab'}, use_global_device_ids=true, to_apply=%region_1.2 | all-reduce | flops 4096 | bytes 32768 | tf_op jit(solution)/shard_map/psum | solution.py:213
  (255 shorter events, 56.6 us)
Async XLA Ops:
  0.6 32.1 %copy-start = (f32[8,4]{0,1:T(4,128)S(1)}, f32[8,4]{0,1:T(4,128)}, u32[]{:S(2)}) copy-start(f32[8,4]{0,1:T(4,128)} %param.25) | copy-start | bytes 388
  0.6 7.1 %copy-start.17 = (bf16[27,64,64]{2,1,0:T(8,128)(2,1)S(1)}, bf16[27,64,64]{2,1,0:T(8,128)(2,1)}, u32[]{:S(2)}) copy-start(bf16[27,64,64]{2,1,0:T(8,128)(2,1)} %param.19) | copy-start | bytes 663556
  0.7 5.6 %collective-permute-start.1 = (bf16[64,1,2048]{2,0,1:T(8,128)(2,1)}, bf16[64,1,2048]{2,0,1:T(8,128)(2,1)S(1)}, u32[]{:S(2)}, u32[]{:S(2)}) collective-permute-start(bf16[64,1,2048]{2,0,1:T(8,128)(2,1)} %param.18), channel_id=1, source_target_pairs={{1,0},{2,1},{3,2},{4,3},{5,4},{6,5},{7,6},{8,7},{9,8},{10,9},{11,1... | collective-permute-start | bytes 786440 | tf_op jit(solution)/shard_map/ppermute | solution.py:25
  2.1 4.4 %collective-permute-start = (bf16[64,1,2048]{2,0,1:T(8,128)(2,1)}, bf16[64,1,2048]{2,0,1:T(8,128)(2,1)S(1)}, u32[]{:S(2)}, u32[]{:S(2)}) collective-permute-start(bf16[64,1,2048]{2,0,1:T(8,128)(2,1)} %param.18), channel_id=1, source_target_pairs={{0,1},{1,2},{2,3},{3,4},{4,5},{5,6},{6,7},{7,8},{8,9},{9,10},{10,1... | collective-permute-start | bytes 786440 | tf_op jit(solution)/shard_map/ppermute | solution.py:22
  14.9 19.0 %copy-start.16 = (bf16[27,64,64]{2,1,0:T(8,128)(2,1)S(1)}, bf16[27,64,64]{2,1,0:T(8,128)(2,1)}, u32[]{:S(2)}) copy-start(bf16[27,64,64]{2,1,0:T(8,128)(2,1)} %param.20) | copy-start | bytes 663556
  15.2 18.2 %collective-permute-start.3 = (bf16[64,1,2048]{2,0,1:T(8,128)(2,1)S(1)}, bf16[64,1,2048]{2,0,1:T(8,128)(2,1)S(1)}, u32[]{:S(2)}, u32[]{:S(2)}) collective-permute-start(bf16[64,1,2048]{2,0,1:T(8,128)(2,1)S(1)} %bitcast.576), channel_id=1, source_target_pairs={{1,0},{2,1},{3,2},{4,3},{5,4},{6,5},{7,6},{8,7},{9,8},{10,9},{11,1... | collective-permute-start | bytes 786440 | tf_op jit(solution)/shard_map/ppermute | solution.py:25
  16.5 16.9 %collective-permute-start.2 = (bf16[64,1,2048]{2,0,1:T(8,128)(2,1)S(1)}, bf16[64,1,2048]{2,0,1:T(8,128)(2,1)S(1)}, u32[]{:S(2)}, u32[]{:S(2)}) collective-permute-start(bf16[64,1,2048]{2,0,1:T(8,128)(2,1)S(1)} %bitcast.577), channel_id=1, source_target_pairs={{0,1},{1,2},{2,3},{3,4},{4,5},{5,6},{6,7},{7,8},{8,9},{9,10},{10,1... | collective-permute-start | bytes 786440 | tf_op jit(solution)/shard_map/ppermute | solution.py:22
  25.7 34.2 %collective-permute-start.9 = (bf16[4,64,128]{2,1,0:T(8,128)(2,1)S(1)}, bf16[4,64,128]{2,1,0:T(8,128)(2,1)S(1)}, u32[]{:S(2)}, u32[]{:S(2)}) collective-permute-start(bf16[4,64,128]{2,1,0:T(8,128)(2,1)S(1)} %get-tuple-element.81), channel_id=1, source_target_pairs={{0,8},{1,9},{2,10},{3,11},{4,12},{5,13},{6,14},{7,15},{16,24},{17,... | collective-permute-start | bytes 196616 | tf_op jit(solution)/shard_map/ppermute | solution.py:43
  31.4 28.6 %collective-permute-start.10 = (bf16[4,64,128]{2,1,0:T(8,128)(2,1)S(1)}, bf16[4,64,128]{2,1,0:T(8,128)(2,1)S(1)}, u32[]{:S(2)}, u32[]{:S(2)}) collective-permute-start(bf16[4,64,128]{2,1,0:T(8,128)(2,1)S(1)} %get-tuple-element.82), channel_id=1, source_target_pairs={{8,0},{9,1},{10,2},{11,3},{12,4},{13,5},{14,6},{15,7},{24,16},{25,... | collective-permute-start | bytes 196616 | tf_op jit(solution)/shard_map/ppermute | solution.py:43
  40.7 5.9 %copy-start.18 = (s32[8,3]{0,1:T(4,128)S(1)}, s32[8,3]{0,1:T(4,128)}, u32[]{:S(2)}) copy-start(s32[8,3]{0,1:T(4,128)} %param.26) | copy-start | bytes 292
  40.7 16.0 %copy-start.21 = (s32[3]{0:T(128)S(1)}, s32[3]{0:T(128)}, u32[]{:S(2)}) copy-start(s32[3]{0:T(128)} %constant.246.clone.1) | copy-start | bytes 40
  40.7 21.6 %copy-start.2 = (f32[1,16,64,128]{3,2,1,0:T(8,128)S(1)}, f32[1,16,64,128]{3,2,1,0:T(8,128)}, u32[]{:S(2)}) copy-start(f32[1,16,64,128]{3,2,1,0:T(8,128)} %param.23) | copy-start | bytes 1572868
  41.6 5.0 %collective-permute-start.5 = (bf16[1,2048]{1,0:T(2,128)(2,1)S(1)}, bf16[1,2048]{1,0:T(2,128)(2,1)S(1)}, u32[]{:S(2)}, u32[]{:S(2)}) collective-permute-start(bf16[1,2048]{1,0:T(2,128)(2,1)S(1)} %convert_element_type.266), channel_id=1, source_target_pairs={{1,0},{2,1},{3,2},{4,3},{5,4},{6,5},{7,6},{8,7},{9,8},{10,9},{11,1... | collective-permute-start | bytes 12296 | tf_op jit(solution)/shard_map/ppermute | solution.py:25
  42.9 4.3 %collective-permute-start.4 = (bf16[1,2048]{1,0:T(2,128)(2,1)S(1)}, bf16[1,2048]{1,0:T(2,128)(2,1)S(1)}, u32[]{:S(2)}, u32[]{:S(2)}) collective-permute-start(bf16[1,2048]{1,0:T(2,128)(2,1)S(1)} %convert_element_type.266), channel_id=1, source_target_pairs={{0,1},{1,2},{2,3},{3,4},{4,5},{5,6},{6,7},{7,8},{8,9},{9,10},{10,1... | collective-permute-start | bytes 12296 | tf_op jit(solution)/shard_map/ppermute | solution.py:22
  47.4 6.8 %collective-permute-start.6 = (f32[1,2,2048]{2,1,0:T(2,128)S(1)}, f32[1,2,2048]{2,1,0:T(2,128)S(1)}, u32[]{:S(2)}, u32[]{:S(2)}) collective-permute-start(f32[1,2,2048]{2,1,0:T(2,128)S(1)} %pad_maximum_fusion.12), channel_id=1, source_target_pairs={{0,1},{1,0},{2,3},{3,2},{4,5},{5,4},{6,7},{7,6},{8,9},{9,8},{10,11... | collective-permute-start | bytes 49160 | tf_op jit(solution)/shard_map/ppermute | solution.py:33
  54.2 5.8 %collective-permute-start.7 = (f32[2,2,2048]{2,1,0:T(2,128)S(1)}, f32[2,2,2048]{2,1,0:T(2,128)S(1)}, u32[]{:S(2)}, u32[]{:S(2)}) collective-permute-start(f32[2,2,2048]{2,1,0:T(2,128)S(1)} %maximum_select_fusion.2), channel_id=1, source_target_pairs={{0,2},{1,3},{2,0},{3,1},{4,6},{5,7},{6,4},{7,5},{8,10},{9,11},{10,... | collective-permute-start | bytes 98312 | tf_op jit(solution)/shard_map/ppermute | solution.py:33
  60.0 5.3 %copy-start.11 = (f32[4,64,128]{2,1,0:T(8,128)}, f32[4,64,128]{2,1,0:T(8,128)S(1)}, u32[]{:S(2)}) copy-start(f32[4,64,128]{2,1,0:T(8,128)S(1)} %convert_element_type.271) | copy-start | bytes 393220
  60.1 4.5 %collective-permute-start.8 = (f32[4,2,2048]{2,1,0:T(2,128)S(1)}, f32[4,2,2048]{2,1,0:T(2,128)S(1)}, u32[]{:S(2)}, u32[]{:S(2)}) collective-permute-start(f32[4,2,2048]{2,1,0:T(2,128)S(1)} %maximum_select_fusion.1), channel_id=1, source_target_pairs={{0,4},{1,5},{2,6},{3,7},{4,0},{5,1},{6,2},{7,3},{8,12},{9,13},{10,... | collective-permute-start | bytes 196616 | tf_op jit(solution)/shard_map/ppermute | solution.py:33
  78.6 4.4 %copy-start.3 = (f32[16,64,128]{2,1,0:T(8,128)}, f32[16,64,128]{2,1,0:T(8,128)S(1)}, u32[]{:S(2)}) copy-start(f32[16,64,128]{2,1,0:T(8,128)S(1)} %copy.59) | copy-start | bytes 1572868
  85.7 7.1 %collective-permute-start.11 = (bf16[4,64,128]{2,1,0:T(8,128)(2,1)S(1)}, bf16[4,64,128]{2,1,0:T(8,128)(2,1)S(1)}, u32[]{:S(2)}, u32[]{:S(2)}) collective-permute-start(bf16[4,64,128]{2,1,0:T(8,128)(2,1)S(1)} %get-tuple-element.79), channel_id=1, source_target_pairs={{0,8},{1,9},{2,10},{3,11},{4,12},{5,13},{6,14},{7,15},{16,24},{17,... | collective-permute-start | bytes 196616 | tf_op jit(solution)/shard_map/ppermute | solution.py:43
  90.8 7.1 %collective-permute-start.12 = (bf16[4,64,128]{2,1,0:T(8,128)(2,1)S(1)}, bf16[4,64,128]{2,1,0:T(8,128)(2,1)S(1)}, u32[]{:S(2)}, u32[]{:S(2)}) collective-permute-start(bf16[4,64,128]{2,1,0:T(8,128)(2,1)S(1)} %get-tuple-element.80), channel_id=1, source_target_pairs={{8,0},{9,1},{10,2},{11,3},{12,4},{13,5},{14,6},{15,7},{24,16},{25,... | collective-permute-start | bytes 196616 | tf_op jit(solution)/shard_map/ppermute | solution.py:43
  106.1 5.3 %collective-permute-start.13 = (bf16[4,64,128]{2,1,0:T(8,128)(2,1)S(1)}, bf16[4,64,128]{2,1,0:T(8,128)(2,1)S(1)}, u32[]{:S(2)}, u32[]{:S(2)}) collective-permute-start(bf16[4,64,128]{2,1,0:T(8,128)(2,1)S(1)} %get-tuple-element.77), channel_id=1, source_target_pairs={{0,8},{1,9},{2,10},{3,11},{4,12},{5,13},{6,14},{7,15},{16,24},{17,... | collective-permute-start | bytes 196616 | tf_op jit(solution)/shard_map/ppermute | solution.py:43
  107.7 7.1 %collective-permute-start.14 = (bf16[4,64,128]{2,1,0:T(8,128)(2,1)S(1)}, bf16[4,64,128]{2,1,0:T(8,128)(2,1)S(1)}, u32[]{:S(2)}, u32[]{:S(2)}) collective-permute-start(bf16[4,64,128]{2,1,0:T(8,128)(2,1)S(1)} %get-tuple-element.78), channel_id=1, source_target_pairs={{8,0},{9,1},{10,2},{11,3},{12,4},{13,5},{14,6},{15,7},{24,16},{25,... | collective-permute-start | bytes 196616 | tf_op jit(solution)/shard_map/ppermute | solution.py:43
  120.1 7.1 %copy-start.5 = (f32[16,64,64,2]{2,0,1,3:T(8,128)S(1)}, f32[16,64,64,2]{2,0,1,3:T(8,128)}, u32[]{:S(2)}) copy-start(f32[16,64,64,2]{2,0,1,3:T(8,128)} %get-tuple-element.63) | copy-start | bytes 1572868
  123.0 11.6 %collective-permute-start.15 = (bf16[4,64,128]{2,1,0:T(8,128)(2,1)S(1)}, bf16[4,64,128]{2,1,0:T(8,128)(2,1)S(1)}, u32[]{:S(2)}, u32[]{:S(2)}) collective-permute-start(bf16[4,64,128]{2,1,0:T(8,128)(2,1)S(1)} %get-tuple-element.75), channel_id=1, source_target_pairs={{0,8},{1,9},{2,10},{3,11},{4,12},{5,13},{6,14},{7,15},{16,24},{17,... | collective-permute-start | bytes 196616 | tf_op jit(solution)/shard_map/ppermute | solution.py:43
  125.2 9.4 %collective-permute-start.16 = (bf16[4,64,128]{2,1,0:T(8,128)(2,1)S(1)}, bf16[4,64,128]{2,1,0:T(8,128)(2,1)S(1)}, u32[]{:S(2)}, u32[]{:S(2)}) collective-permute-start(bf16[4,64,128]{2,1,0:T(8,128)(2,1)S(1)} %get-tuple-element.76), channel_id=1, source_target_pairs={{8,0},{9,1},{10,2},{11,3},{12,4},{13,5},{14,6},{15,7},{24,16},{25,... | collective-permute-start | bytes 196616 | tf_op jit(solution)/shard_map/ppermute | solution.py:43
  147.4 81.3 %copy-start.1 = (f32[8,4]{0,1:T(4,128)S(1)}, f32[8,4]{0,1:T(4,128)}, u32[]{:S(2)}) copy-start(f32[8,4]{0,1:T(4,128)} %param.25) | copy-start | bytes 388
  148.5 6.8 %collective-permute-start.18 = (f32[1,2048]{1,0:T(1,128)S(1)}, f32[1,2048]{1,0:T(1,128)S(1)}, u32[]{:S(2)}, u32[]{:S(2)}) collective-permute-start(f32[1,2048]{1,0:T(1,128)S(1)} %get-tuple-element.91), channel_id=1, source_target_pairs={{0,8},{1,9},{2,10},{3,11},{4,12},{5,13},{6,14},{7,15},{16,24},{17,... | collective-permute-start | bytes 24584 | tf_op jit(solution)/shard_map/ppermute | solution.py:43
  153.9 6.4 %collective-permute-start.17 = (f32[1,2048]{1,0:T(1,128)S(1)}, f32[1,2048]{1,0:T(1,128)S(1)}, u32[]{:S(2)}, u32[]{:S(2)}) collective-permute-start(f32[1,2048]{1,0:T(1,128)S(1)} %get-tuple-element.92), channel_id=1, source_target_pairs={{8,0},{9,1},{10,2},{11,3},{12,4},{13,5},{14,6},{15,7},{24,16},{25,... | collective-permute-start | bytes 24584 | tf_op jit(solution)/shard_map/ppermute | solution.py:43
  160.5 4.0 %collective-permute-start.19 = (f32[4,1,2048]{2,0,1:T(4,128)S(1)}, f32[4,1,2048]{2,0,1:T(4,128)S(1)}, u32[]{:S(2)}, u32[]{:S(2)}) collective-permute-start(f32[4,1,2048]{2,0,1:T(4,128)S(1)} %select_bitcast_fusion), channel_id=1, source_target_pairs={{0,4},{1,5},{2,6},{3,7},{4,0},{5,1},{6,2},{7,3},{8,12},{9,13},{10,... | collective-permute-start | bytes 98312 | tf_op jit(solution)/shard_map/ppermute | solution.py:33
  164.5 3.8 %collective-permute-start.20 = (f32[2,1,2048]{2,0,1:T(2,128)S(1)}, f32[2,1,2048]{2,0,1:T(2,128)S(1)}, u32[]{:S(2)}, u32[]{:S(2)}) collective-permute-start(f32[2,1,2048]{2,0,1:T(2,128)S(1)} %broadcast_select_fusion.4), channel_id=1, source_target_pairs={{0,2},{1,3},{2,0},{3,1},{4,6},{5,7},{6,4},{7,5},{8,10},{9,11},{10,... | collective-permute-start | bytes 49160 | tf_op jit(solution)/shard_map/ppermute | solution.py:33
  168.3 59.8 %collective-permute-start.21 = (f32[1,1,2048]{2,0,1:T(1,128)S(1)}, f32[1,1,2048]{2,0,1:T(1,128)S(1)}, u32[]{:S(2)}, u32[]{:S(2)}) collective-permute-start(f32[1,1,2048]{2,0,1:T(1,128)S(1)} %broadcast_select_fusion.5), channel_id=1, source_target_pairs={{0,1},{1,0},{2,3},{3,2},{4,5},{5,4},{6,7},{7,6},{8,9},{9,8},{10,11... | collective-permute-start | bytes 24584 | tf_op jit(solution)/shard_map/ppermute | solution.py:33
  (13 other events, 19.8 us)
where the time goes:
time: 230 us; the launch traced here: 229 us
  blocking collectives  59.7 us (26%)
  starting transfers between devices  56.9 us (25%)
  local copies, waits for them, and re-layouts  31.1 us (14%)
  other arithmetic  28.9 us (13%)
  waiting for transfers between devices  20.4 us (9%)
  between operations  16.9 us (7%)
  matrix products  14.7 us (6%)
    psum x1, blocking collectives, body(): traces = lax.psum(own_traces, 'slab')  59.7 us
    ppermute x10, starting transfers between devices, from_behind(): lax.ppermute(value, axis, [(source, source + steps) for source in range(l...  26.7 us
    ppermute x3, starting transfers between devices, extended_2(): lax.ppermute(lax.slice_in_dim(block, block.shape[dim] - width, None, axis...  15.9 us
    dot_general x54, matrix products, conv_taps(): jnp.einsum('oi,izn->ozn', weight[tap_index], piece * column_valid, prefer...  14.4 us
    ppermute x10, waiting for transfers between devices, from_behind(): lax.ppermute(value, axis, [(source, source + steps) for source in range(l...  14.1 us
    add x4, other arithmetic, body(): advanced = 2.0 * current - previous + courant_sq * laplace_term  12.9 us
    ppermute x6, starting transfers between devices, from_partner(): return lax.ppermute(value, axis, pairs)  10.4 us
    gather x4, local copies, waits for them, and re-layouts, body(): advanced[station_depth, station[1], station[2]]  5.93 us
  transfers between devices with their start and end apart: 22, of which 9 were waited for; matrix products, arithmetic and copies ran while one was open for 10% of the time, Pallas kernels for 0%

commit v1 on v0

--- a/solution.py
+++ b/solution.py
@@ -210,7 +210,7 @@
         previous, current = (current, advanced)
     record = jnp.stack(samples_list)
     own_traces = jnp.where((jnp.arange(SHOTS) == my_shot)[:, None, None], record[None], 0.0)
-    traces = lax.psum(own_traces, "slab")
+    traces = jnp.sum(lax.all_gather(own_traces, "slab"), axis=0)
     fine_gradient = 2.0 * courant * courant * fine_speed * correlation
     shape_holder = jnp.zeros((slab_planes + 2, velocity.shape[1]), jnp.float32)
     unused, pullback = jax.vjp(upsample_slab, shape_holder)

time: 230 us -> 191 us (0.83)
  blocking collectives: 59.7 us -> 19.9 us
    psum x1 -> x0, blocking collectives: 59.7 us -> none  [body(): traces = lax.psum(own_traces, 'slab')]
    all_gather x0 -> x1, blocking collectives: none -> 19.9 us  [body(): traces = jnp.sum(lax.all_gather(own_traces, 'slab'), axis=0)]
  transfers between devices with their start and end apart: 22 -> 22, of which waited for: 9 -> 9; matrix products, arithmetic and copies ran while one was open for 10% -> 12% of each run, Pallas kernels for 0% -> 0%
where the time goes in v1:
time: 191 us; the launch traced here: 190 us
  starting transfers between devices  56.9 us (30%)
  local copies, waits for them, and re-layouts  31.8 us (17%)
  other arithmetic  28.9 us (15%)
  waiting for transfers between devices  20.4 us (11%)
  blocking collectives  19.9 us (10%)
  between operations  16.9 us (9%)
  matrix products  14.7 us (8%)
    ppermute x10, starting transfers between devices, from_behind(): lax.ppermute(value, axis, [(source, source + steps) for source in range(l...  26.7 us
    all_gather x1, blocking collectives, body(): traces = jnp.sum(lax.all_gather(own_traces, 'slab'), axis=0)  19.9 us
    ppermute x3, starting transfers between devices, extended_2(): lax.ppermute(lax.slice_in_dim(block, block.shape[dim] - width, None, axis...  15.9 us
    dot_general x54, matrix products, conv_taps(): jnp.einsum('oi,izn->ozn', weight[tap_index], piece * column_valid, prefer...  14.4 us
    ppermute x10, waiting for transfers between devices, from_behind(): lax.ppermute(value, axis, [(source, source + steps) for source in range(l...  14.1 us
    add x4, other arithmetic, body(): advanced = 2.0 * current - previous + courant_sq * laplace_term  12.9 us
    ppermute x6, starting transfers between devices, from_partner(): return lax.ppermute(value, axis, pairs)  10.4 us
    gather x4, local copies, waits for them, and re-layouts, body(): advanced[station_depth, station[1], station[2]]  5.93 us
  transfers between devices with their start and end apart: 22, of which 9 were waited for; matrix products, arithmetic and copies ran while one was open for 12% of the time, Pallas kernels for 0%

profile of v1, /device:TPU:0, one launch (start us, length us, event | category | flops | bytes accessed | tf_op | source)
XLA Modules:
  0.0 189.6 jit_solution(3988379704570082587)
XLA Ops:
  2.1 3.1 %collective-permute-start = (bf16[64,1,2048]{2,0,1:T(8,128)(2,1)}, bf16[64,1,2048]{2,0,1:T(8,128)(2,1)S(1)}, u32[]{:S(2)}, u32[]{:S(2)}) collective-permute-start(bf16[64,1,2048]{2,0,1:T(8,128)(2,1)} %param.18), channel_id=1, source_target_pairs={{0,1},{1,2},{2,3},{3,4},{4,5},{5,6},{6,7},{7,8},{8,9},{9,10},{10,1... | collective-permute-start | bytes 786440 | tf_op jit(solution)/shard_map/ppermute | solution.py:22
  16.5 9.2 %collective-permute-start.2 = (bf16[64,1,2048]{2,0,1:T(8,128)(2,1)S(1)}, bf16[64,1,2048]{2,0,1:T(8,128)(2,1)S(1)}, u32[]{:S(2)}, u32[]{:S(2)}) collective-permute-start(bf16[64,1,2048]{2,0,1:T(8,128)(2,1)S(1)} %bitcast.577), channel_id=1, source_target_pairs={{0,1},{1,2},{2,3},{3,4},{4,5},{5,6},{6,7},{7,8},{8,9},{9,10},{10,1... | collective-permute-start | bytes 786440 | tf_op jit(solution)/shard_map/ppermute | solution.py:22
  25.7 5.7 %collective-permute-start.9 = (bf16[4,64,128]{2,1,0:T(8,128)(2,1)S(1)}, bf16[4,64,128]{2,1,0:T(8,128)(2,1)S(1)}, u32[]{:S(2)}, u32[]{:S(2)}) collective-permute-start(bf16[4,64,128]{2,1,0:T(8,128)(2,1)S(1)} %get-tuple-element.84), channel_id=1, source_target_pairs={{0,8},{1,9},{2,10},{3,11},{4,12},{5,13},{6,14},{7,15},{16,24},{17,... | collective-permute-start | bytes 196616 | tf_op jit(solution)/shard_map/ppermute | solution.py:43
  42.9 3.6 %collective-permute-start.4 = (bf16[1,2048]{1,0:T(2,128)(2,1)S(1)}, bf16[1,2048]{1,0:T(2,128)(2,1)S(1)}, u32[]{:S(2)}, u32[]{:S(2)}) collective-permute-start(bf16[1,2048]{1,0:T(2,128)(2,1)S(1)} %convert_element_type.266), channel_id=1, source_target_pairs={{0,1},{1,2},{2,3},{3,4},{4,5},{5,6},{6,7},{7,8},{8,9},{9,10},{10,1... | collective-permute-start | bytes 12296 | tf_op jit(solution)/shard_map/ppermute | solution.py:22
  47.4 1.8 collective-permute-start.6
  54.2 2.4 %collective-permute-start.7 = (f32[2,2,2048]{2,1,0:T(2,128)S(1)}, f32[2,2,2048]{2,1,0:T(2,128)S(1)}, u32[]{:S(2)}, u32[]{:S(2)}) collective-permute-start(f32[2,2,2048]{2,1,0:T(2,128)S(1)} %maximum_select_fusion.2), channel_id=1, source_target_pairs={{0,2},{1,3},{2,0},{3,1},{4,6},{5,7},{6,4},{7,5},{8,10},{9,11},{10,... | collective-permute-start | bytes 98312 | tf_op jit(solution)/shard_map/ppermute | solution.py:33
  60.1 2.2 %collective-permute-start.8 = (f32[4,2,2048]{2,1,0:T(2,128)S(1)}, f32[4,2,2048]{2,1,0:T(2,128)S(1)}, u32[]{:S(2)}, u32[]{:S(2)}) collective-permute-start(f32[4,2,2048]{2,1,0:T(2,128)S(1)} %maximum_select_fusion.1), channel_id=1, source_target_pairs={{0,4},{1,5},{2,6},{3,7},{4,0},{5,1},{6,2},{7,3},{8,12},{9,13},{10,... | collective-permute-start | bytes 196616 | tf_op jit(solution)/shard_map/ppermute | solution.py:33
  62.8 1.7 collective-permute-done.8
  72.2 1.7 fusion.155
  75.1 1.9 %copy.110 = f32[16,64,64,2]{1,0,3,2:T(8,128)} copy(f32[16,64,64,2]{2,0,1,3:T(8,128)S(1)} %get-tuple-element.67) | data formatting | bytes 1048576 | tf_op jit(solution)/shard_map/integer_pow | solution.py:182
  77.0 1.6 copy.111
  78.6 4.4 %fusion.164 = (f32[16,64,128]{2,1,0:T(8,128)S(1)}, f32[16,64,128]{2,1,0:T(8,128)}) fusion(f32[1,16,64,128]{3,2,1,0:T(8,128)} %param.22, f32[16,64,128]{2,1,0:T(8,128)S(1)} %copy.111, f32[1,16,64,128]{3,2,1,0:T(8,128)S(1)} %copy-done.2, f32[24,72,136]{2,1,0:T(8,128)S(1)} %select_maximum_fusion.6, f32[4,64,128]{2,1,0:T(8,128)} %copy-done.11, ...), kind=kLoop, calls=%fused_computation.321 | loop fusion | flops 5373952 | bytes 11796480 | tf_op jit(solution)/shard_map/add | solution.py:203
  85.7 5.2 %collective-permute-start.11 = (bf16[4,64,128]{2,1,0:T(8,128)(2,1)S(1)}, bf16[4,64,128]{2,1,0:T(8,128)(2,1)S(1)}, u32[]{:S(2)}, u32[]{:S(2)}) collective-permute-start(bf16[4,64,128]{2,1,0:T(8,128)(2,1)S(1)} %get-tuple-element.82), channel_id=1, source_target_pairs={{0,8},{1,9},{2,10},{3,11},{4,12},{5,13},{6,14},{7,15},{16,24},{17,... | collective-permute-start | bytes 196616 | tf_op jit(solution)/shard_map/ppermute | solution.py:43
  92.7 5.2 %collective-permute-done.12 = bf16[4,64,128]{2,1,0:T(8,128)(2,1)S(1)} collective-permute-done((bf16[4,64,128]{2,1,0:T(8,128)(2,1)S(1)}, bf16[4,64,128]{2,1,0:T(8,128)(2,1)S(1)}, u32[]{:S(2)}, u32[]{:S(2)}) %collective-permute-start.12) | collective-permute-done | bytes 65568 | tf_op jit(solution)/shard_map/ppermute | solution.py:43
  99.1 4.2 %multiply_add_fusion.2 = (f32[16,64,128]{2,1,0:T(8,128)S(1)}, f32[16,64,128]{2,1,0:T(8,128)}) fusion(f32[16,64,128]{2,1,0:T(8,128)} %copy-done.3, f32[16,64,128]{2,1,0:T(8,128)S(1)} %scatter-add.14, f32[1,16,64,128]{3,2,1,0:T(8,128)S(1)} %copy-done.2, f32[24,72,136]{2,1,0:T(8,128)S(1)} %select_maximum_fusion.4, f32[4,64,128]{2,1,0:T(8,128)} %copy-done.13, ...), kind=kLoop, calls=%fused_computation.326 | loop fusion | flops 5373952 | bytes 11272192 | tf_op jit(solution)/shard_map/add | solution.py:203
  106.1 1.6 collective-permute-start.13
  107.7 1.5 collective-permute-start.14
  110.0 1.5 gather_fusion
  111.5 3.3 %collective-permute-done.14 = bf16[4,64,128]{2,1,0:T(8,128)(2,1)S(1)} collective-permute-done((bf16[4,64,128]{2,1,0:T(8,128)(2,1)S(1)}, bf16[4,64,128]{2,1,0:T(8,128)(2,1)S(1)}, u32[]{:S(2)}, u32[]{:S(2)}) %collective-permute-start.14) | collective-permute-done | bytes 65568 | tf_op jit(solution)/shard_map/ppermute | solution.py:43
  116.0 4.2 %multiply_add_fusion.1 = (f32[16,64,128]{2,1,0:T(8,128)S(1)}, f32[16,64,128]{2,1,0:T(8,128)}) fusion(f32[16,64,128]{2,1,0:T(8,128)} %copy-done.3, f32[16,64,128]{2,1,0:T(8,128)S(1)} %scatter-add.14, f32[16,64,128]{2,1,0:T(8,128)S(1)} %scatter-add.15, f32[24,72,136]{2,1,0:T(8,128)S(1)} %select_maximum_fusion.2, f32[4,64,128]{2,1,0:T(8,128)} %copy-done.12, ...), kind=kLoop, calls=%fused_computation.325 | loop fusion | flops 5373952 | bytes 11272192 | tf_op jit(solution)/shard_map/add | solution.py:203
  123.0 2.2 %collective-permute-start.15 = (bf16[4,64,128]{2,1,0:T(8,128)(2,1)S(1)}, bf16[4,64,128]{2,1,0:T(8,128)(2,1)S(1)}, u32[]{:S(2)}, u32[]{:S(2)}) collective-permute-start(bf16[4,64,128]{2,1,0:T(8,128)(2,1)S(1)} %get-tuple-element.78), channel_id=1, source_target_pairs={{0,8},{1,9},{2,10},{3,11},{4,12},{5,13},{6,14},{7,15},{16,24},{17,... | collective-permute-start | bytes 196616 | tf_op jit(solution)/shard_map/ppermute | solution.py:43
  127.2 2.0 %copy.115 = f32[16,64,64,2]{1,0,3,2:T(8,128)} copy(f32[16,64,64,2]{2,0,1,3:T(8,128)S(1)} %copy-done.5) | data formatting | bytes 1048576 | tf_op jit(solution)/shard_map/mul | solution.py:214
  129.2 2.4 %copy.116 = f32[16,64,128]{2,1,0:T(8,128)} copy(f32[16,64,128]{1,0,2:T(8,128)} %bitcast.569) | data formatting | bytes 1048576 | tf_op jit(solution)/shard_map/mul | solution.py:214
  136.0 3.4 %fusion.158 = (f32[16,64,128]{2,1,0:T(8,128)}, f32[16,64,128]{2,1,0:T(8,128)S(1)}) fusion(f32[16,64,128]{2,1,0:T(8,128)S(1)} %copy-done.10, f32[16,64,128]{2,1,0:T(8,128)S(1)} %copy-done.9, f32[16,64,128]{2,1,0:T(8,128)S(1)} %copy-done.8, f32[16,64,128]{2,1,0:T(8,128)S(1)} %copy-done.7, bf16[4,1,16,64,128]{4,3,2,1,0:T(8,128)(2,1)S(1)} %copy-done.14, ...), kind=kLoop, calls=%fused_computation.310 | loop fusion | flops 6422528 | bytes 13369344 | tf_op jit(solution)/shard_map/mul | solution.py:214
  143.7 1.5 copy.117
  148.5 5.4 %collective-permute-start.18 = (f32[1,2048]{1,0:T(1,128)S(1)}, f32[1,2048]{1,0:T(1,128)S(1)}, u32[]{:S(2)}, u32[]{:S(2)}) collective-permute-start(f32[1,2048]{1,0:T(1,128)S(1)} %get-tuple-element.94), channel_id=1, source_target_pairs={{0,8},{1,9},{2,10},{3,11},{4,12},{5,13},{6,14},{7,15},{16,24},{17,... | collective-permute-start | bytes 24584 | tf_op jit(solution)/shard_map/ppermute | solution.py:43
  155.3 5.1 %collective-permute-done.17 = f32[1,2048]{1,0:T(1,128)S(1)} collective-permute-done((f32[1,2048]{1,0:T(1,128)S(1)}, f32[1,2048]{1,0:T(1,128)S(1)}, u32[]{:S(2)}, u32[]{:S(2)}) %collective-permute-start.17) | collective-permute-done | bytes 8224 | tf_op jit(solution)/shard_map/ppermute | solution.py:43
  160.5 2.1 %collective-permute-start.19 = (f32[4,1,2048]{2,0,1:T(4,128)S(1)}, f32[4,1,2048]{2,0,1:T(4,128)S(1)}, u32[]{:S(2)}, u32[]{:S(2)}) collective-permute-start(f32[4,1,2048]{2,0,1:T(4,128)S(1)} %select_bitcast_fusion), channel_id=1, source_target_pairs={{0,4},{1,5},{2,6},{3,7},{4,0},{5,1},{6,2},{7,3},{8,12},{9,13},{10,... | collective-permute-start | bytes 98312 | tf_op jit(solution)/shard_map/ppermute | solution.py:33
  162.6 1.9 collective-permute-done.19
  164.5 1.8 collective-permute-start.20
  166.4 2.0 %collective-permute-done.20 = f32[2,1,2048]{2,0,1:T(2,128)S(1)} collective-permute-done((f32[2,1,2048]{2,0,1:T(2,128)S(1)}, f32[2,1,2048]{2,0,1:T(2,128)S(1)}, u32[]{:S(2)}, u32[]{:S(2)}) %collective-permute-start.20) | collective-permute-done | bytes 16416 | tf_op jit(solution)/shard_map/ppermute | solution.py:33
  168.4 19.9 %all_gather.4 = f32[16,8,4,128]{3,1,2,0:T(8,128)S(1)} all-gather(f32[1,8,4,128]{3,1,2,0:T(8,128)S(1)} %broadcast_select_fusion.9), channel_id=1, replica_groups=mesh['groups'=2,'slab'=16] {'slab'}, dimensions={0}, use_global_device_ids=true | all-gather | bytes 278528 | tf_op jit(solution)/shard_map/all_gather | solution.py:213
  (257 shorter events, 57.3 us)
Async XLA Ops:
  0.6 32.1 %copy-start = (f32[8,4]{0,1:T(4,128)S(1)}, f32[8,4]{0,1:T(4,128)}, u32[]{:S(2)}) copy-start(f32[8,4]{0,1:T(4,128)} %param.25) | copy-start | bytes 388
  0.6 7.1 %copy-start.17 = (bf16[27,64,64]{2,1,0:T(8,128)(2,1)S(1)}, bf16[27,64,64]{2,1,0:T(8,128)(2,1)}, u32[]{:S(2)}) copy-start(bf16[27,64,64]{2,1,0:T(8,128)(2,1)} %param.19) | copy-start | bytes 663556
  0.7 5.6 %collective-permute-start.1 = (bf16[64,1,2048]{2,0,1:T(8,128)(2,1)}, bf16[64,1,2048]{2,0,1:T(8,128)(2,1)S(1)}, u32[]{:S(2)}, u32[]{:S(2)}) collective-permute-start(bf16[64,1,2048]{2,0,1:T(8,128)(2,1)} %param.18), channel_id=1, source_target_pairs={{1,0},{2,1},{3,2},{4,3},{5,4},{6,5},{7,6},{8,7},{9,8},{10,9},{11,1... | collective-permute-start | bytes 786440 | tf_op jit(solution)/shard_map/ppermute | solution.py:25
  2.1 4.4 %collective-permute-start = (bf16[64,1,2048]{2,0,1:T(8,128)(2,1)}, bf16[64,1,2048]{2,0,1:T(8,128)(2,1)S(1)}, u32[]{:S(2)}, u32[]{:S(2)}) collective-permute-start(bf16[64,1,2048]{2,0,1:T(8,128)(2,1)} %param.18), channel_id=1, source_target_pairs={{0,1},{1,2},{2,3},{3,4},{4,5},{5,6},{6,7},{7,8},{8,9},{9,10},{10,1... | collective-permute-start | bytes 786440 | tf_op jit(solution)/shard_map/ppermute | solution.py:22
  14.9 19.0 %copy-start.16 = (bf16[27,64,64]{2,1,0:T(8,128)(2,1)S(1)}, bf16[27,64,64]{2,1,0:T(8,128)(2,1)}, u32[]{:S(2)}) copy-start(bf16[27,64,64]{2,1,0:T(8,128)(2,1)} %param.20) | copy-start | bytes 663556
  15.2 18.2 %collective-permute-start.3 = (bf16[64,1,2048]{2,0,1:T(8,128)(2,1)S(1)}, bf16[64,1,2048]{2,0,1:T(8,128)(2,1)S(1)}, u32[]{:S(2)}, u32[]{:S(2)}) collective-permute-start(bf16[64,1,2048]{2,0,1:T(8,128)(2,1)S(1)} %bitcast.576), channel_id=1, source_target_pairs={{1,0},{2,1},{3,2},{4,3},{5,4},{6,5},{7,6},{8,7},{9,8},{10,9},{11,1... | collective-permute-start | bytes 786440 | tf_op jit(solution)/shard_map/ppermute | solution.py:25
  16.5 16.9 %collective-permute-start.2 = (bf16[64,1,2048]{2,0,1:T(8,128)(2,1)S(1)}, bf16[64,1,2048]{2,0,1:T(8,128)(2,1)S(1)}, u32[]{:S(2)}, u32[]{:S(2)}) collective-permute-start(bf16[64,1,2048]{2,0,1:T(8,128)(2,1)S(1)} %bitcast.577), channel_id=1, source_target_pairs={{0,1},{1,2},{2,3},{3,4},{4,5},{5,6},{6,7},{7,8},{8,9},{9,10},{10,1... | collective-permute-start | bytes 786440 | tf_op jit(solution)/shard_map/ppermute | solution.py:22
  25.7 34.2 %collective-permute-start.9 = (bf16[4,64,128]{2,1,0:T(8,128)(2,1)S(1)}, bf16[4,64,128]{2,1,0:T(8,128)(2,1)S(1)}, u32[]{:S(2)}, u32[]{:S(2)}) collective-permute-start(bf16[4,64,128]{2,1,0:T(8,128)(2,1)S(1)} %get-tuple-element.84), channel_id=1, source_target_pairs={{0,8},{1,9},{2,10},{3,11},{4,12},{5,13},{6,14},{7,15},{16,24},{17,... | collective-permute-start | bytes 196616 | tf_op jit(solution)/shard_map/ppermute | solution.py:43
  31.4 28.6 %collective-permute-start.10 = (bf16[4,64,128]{2,1,0:T(8,128)(2,1)S(1)}, bf16[4,64,128]{2,1,0:T(8,128)(2,1)S(1)}, u32[]{:S(2)}, u32[]{:S(2)}) collective-permute-start(bf16[4,64,128]{2,1,0:T(8,128)(2,1)S(1)} %get-tuple-element.85), channel_id=1, source_target_pairs={{8,0},{9,1},{10,2},{11,3},{12,4},{13,5},{14,6},{15,7},{24,16},{25,... | collective-permute-start | bytes 196616 | tf_op jit(solution)/shard_map/ppermute | solution.py:43
  40.7 5.9 %copy-start.18 = (s32[8,3]{0,1:T(4,128)S(1)}, s32[8,3]{0,1:T(4,128)}, u32[]{:S(2)}) copy-start(s32[8,3]{0,1:T(4,128)} %param.26) | copy-start | bytes 292
  40.7 16.0 %copy-start.21 = (s32[3]{0:T(128)S(1)}, s32[3]{0:T(128)}, u32[]{:S(2)}) copy-start(s32[3]{0:T(128)} %constant.246.clone.1) | copy-start | bytes 40
  40.7 21.6 %copy-start.2 = (f32[1,16,64,128]{3,2,1,0:T(8,128)S(1)}, f32[1,16,64,128]{3,2,1,0:T(8,128)}, u32[]{:S(2)}) copy-start(f32[1,16,64,128]{3,2,1,0:T(8,128)} %param.23) | copy-start | bytes 1572868
  41.6 5.0 %collective-permute-start.5 = (bf16[1,2048]{1,0:T(2,128)(2,1)S(1)}, bf16[1,2048]{1,0:T(2,128)(2,1)S(1)}, u32[]{:S(2)}, u32[]{:S(2)}) collective-permute-start(bf16[1,2048]{1,0:T(2,128)(2,1)S(1)} %convert_element_type.266), channel_id=1, source_target_pairs={{1,0},{2,1},{3,2},{4,3},{5,4},{6,5},{7,6},{8,7},{9,8},{10,9},{11,1... | collective-permute-start | bytes 12296 | tf_op jit(solution)/shard_map/ppermute | solution.py:25
  42.9 4.3 %collective-permute-start.4 = (bf16[1,2048]{1,0:T(2,128)(2,1)S(1)}, bf16[1,2048]{1,0:T(2,128)(2,1)S(1)}, u32[]{:S(2)}, u32[]{:S(2)}) collective-permute-start(bf16[1,2048]{1,0:T(2,128)(2,1)S(1)} %convert_element_type.266), channel_id=1, source_target_pairs={{0,1},{1,2},{2,3},{3,4},{4,5},{5,6},{6,7},{7,8},{8,9},{9,10},{10,1... | collective-permute-start | bytes 12296 | tf_op jit(solution)/shard_map/ppermute | solution.py:22
  47.4 6.8 %collective-permute-start.6 = (f32[1,2,2048]{2,1,0:T(2,128)S(1)}, f32[1,2,2048]{2,1,0:T(2,128)S(1)}, u32[]{:S(2)}, u32[]{:S(2)}) collective-permute-start(f32[1,2,2048]{2,1,0:T(2,128)S(1)} %pad_maximum_fusion.12), channel_id=1, source_target_pairs={{0,1},{1,0},{2,3},{3,2},{4,5},{5,4},{6,7},{7,6},{8,9},{9,8},{10,11... | collective-permute-start | bytes 49160 | tf_op jit(solution)/shard_map/ppermute | solution.py:33
  54.2 5.8 %collective-permute-start.7 = (f32[2,2,2048]{2,1,0:T(2,128)S(1)}, f32[2,2,2048]{2,1,0:T(2,128)S(1)}, u32[]{:S(2)}, u32[]{:S(2)}) collective-permute-start(f32[2,2,2048]{2,1,0:T(2,128)S(1)} %maximum_select_fusion.2), channel_id=1, source_target_pairs={{0,2},{1,3},{2,0},{3,1},{4,6},{5,7},{6,4},{7,5},{8,10},{9,11},{10,... | collective-permute-start | bytes 98312 | tf_op jit(solution)/shard_map/ppermute | solution.py:33
  60.0 5.3 %copy-start.11 = (f32[4,64,128]{2,1,0:T(8,128)}, f32[4,64,128]{2,1,0:T(8,128)S(1)}, u32[]{:S(2)}) copy-start(f32[4,64,128]{2,1,0:T(8,128)S(1)} %convert_element_type.271) | copy-start | bytes 393220
  60.1 4.5 %collective-permute-start.8 = (f32[4,2,2048]{2,1,0:T(2,128)S(1)}, f32[4,2,2048]{2,1,0:T(2,128)S(1)}, u32[]{:S(2)}, u32[]{:S(2)}) collective-permute-start(f32[4,2,2048]{2,1,0:T(2,128)S(1)} %maximum_select_fusion.1), channel_id=1, source_target_pairs={{0,4},{1,5},{2,6},{3,7},{4,0},{5,1},{6,2},{7,3},{8,12},{9,13},{10,... | collective-permute-start | bytes 196616 | tf_op jit(solution)/shard_map/ppermute | solution.py:33
  78.6 4.4 %copy-start.3 = (f32[16,64,128]{2,1,0:T(8,128)}, f32[16,64,128]{2,1,0:T(8,128)S(1)}, u32[]{:S(2)}) copy-start(f32[16,64,128]{2,1,0:T(8,128)S(1)} %copy.111) | copy-start | bytes 1572868
  85.7 7.1 %collective-permute-start.11 = (bf16[4,64,128]{2,1,0:T(8,128)(2,1)S(1)}, bf16[4,64,128]{2,1,0:T(8,128)(2,1)S(1)}, u32[]{:S(2)}, u32[]{:S(2)}) collective-permute-start(bf16[4,64,128]{2,1,0:T(8,128)(2,1)S(1)} %get-tuple-element.82), channel_id=1, source_target_pairs={{0,8},{1,9},{2,10},{3,11},{4,12},{5,13},{6,14},{7,15},{16,24},{17,... | collective-permute-start | bytes 196616 | tf_op jit(solution)/shard_map/ppermute | solution.py:43
  90.8 7.1 %collective-permute-start.12 = (bf16[4,64,128]{2,1,0:T(8,128)(2,1)S(1)}, bf16[4,64,128]{2,1,0:T(8,128)(2,1)S(1)}, u32[]{:S(2)}, u32[]{:S(2)}) collective-permute-start(bf16[4,64,128]{2,1,0:T(8,128)(2,1)S(1)} %get-tuple-element.83), channel_id=1, source_target_pairs={{8,0},{9,1},{10,2},{11,3},{12,4},{13,5},{14,6},{15,7},{24,16},{25,... | collective-permute-start | bytes 196616 | tf_op jit(solution)/shard_map/ppermute | solution.py:43
  106.1 5.3 %collective-permute-start.13 = (bf16[4,64,128]{2,1,0:T(8,128)(2,1)S(1)}, bf16[4,64,128]{2,1,0:T(8,128)(2,1)S(1)}, u32[]{:S(2)}, u32[]{:S(2)}) collective-permute-start(bf16[4,64,128]{2,1,0:T(8,128)(2,1)S(1)} %get-tuple-element.80), channel_id=1, source_target_pairs={{0,8},{1,9},{2,10},{3,11},{4,12},{5,13},{6,14},{7,15},{16,24},{17,... | collective-permute-start | bytes 196616 | tf_op jit(solution)/shard_map/ppermute | solution.py:43
  107.7 7.1 %collective-permute-start.14 = (bf16[4,64,128]{2,1,0:T(8,128)(2,1)S(1)}, bf16[4,64,128]{2,1,0:T(8,128)(2,1)S(1)}, u32[]{:S(2)}, u32[]{:S(2)}) collective-permute-start(bf16[4,64,128]{2,1,0:T(8,128)(2,1)S(1)} %get-tuple-element.81), channel_id=1, source_target_pairs={{8,0},{9,1},{10,2},{11,3},{12,4},{13,5},{14,6},{15,7},{24,16},{25,... | collective-permute-start | bytes 196616 | tf_op jit(solution)/shard_map/ppermute | solution.py:43
  120.1 7.1 %copy-start.5 = (f32[16,64,64,2]{2,0,1,3:T(8,128)S(1)}, f32[16,64,64,2]{2,0,1,3:T(8,128)}, u32[]{:S(2)}) copy-start(f32[16,64,64,2]{2,0,1,3:T(8,128)} %get-tuple-element.66) | copy-start | bytes 1572868
  123.0 11.6 %collective-permute-start.15 = (bf16[4,64,128]{2,1,0:T(8,128)(2,1)S(1)}, bf16[4,64,128]{2,1,0:T(8,128)(2,1)S(1)}, u32[]{:S(2)}, u32[]{:S(2)}) collective-permute-start(bf16[4,64,128]{2,1,0:T(8,128)(2,1)S(1)} %get-tuple-element.78), channel_id=1, source_target_pairs={{0,8},{1,9},{2,10},{3,11},{4,12},{5,13},{6,14},{7,15},{16,24},{17,... | collective-permute-start | bytes 196616 | tf_op jit(solution)/shard_map/ppermute | solution.py:43
  125.2 9.4 %collective-permute-start.16 = (bf16[4,64,128]{2,1,0:T(8,128)(2,1)S(1)}, bf16[4,64,128]{2,1,0:T(8,128)(2,1)S(1)}, u32[]{:S(2)}, u32[]{:S(2)}) collective-permute-start(bf16[4,64,128]{2,1,0:T(8,128)(2,1)S(1)} %get-tuple-element.79), channel_id=1, source_target_pairs={{8,0},{9,1},{10,2},{11,3},{12,4},{13,5},{14,6},{15,7},{24,16},{25,... | collective-permute-start | bytes 196616 | tf_op jit(solution)/shard_map/ppermute | solution.py:43
  147.8 41.8 %copy-start.1 = (f32[8,4]{0,1:T(4,128)S(1)}, f32[8,4]{0,1:T(4,128)}, u32[]{:S(2)}) copy-start(f32[8,4]{0,1:T(4,128)} %param.25) | copy-start | bytes 388
  148.5 6.8 %collective-permute-start.18 = (f32[1,2048]{1,0:T(1,128)S(1)}, f32[1,2048]{1,0:T(1,128)S(1)}, u32[]{:S(2)}, u32[]{:S(2)}) collective-permute-start(f32[1,2048]{1,0:T(1,128)S(1)} %get-tuple-element.94), channel_id=1, source_target_pairs={{0,8},{1,9},{2,10},{3,11},{4,12},{5,13},{6,14},{7,15},{16,24},{17,... | collective-permute-start | bytes 24584 | tf_op jit(solution)/shard_map/ppermute | solution.py:43
  153.9 6.4 %collective-permute-start.17 = (f32[1,2048]{1,0:T(1,128)S(1)}, f32[1,2048]{1,0:T(1,128)S(1)}, u32[]{:S(2)}, u32[]{:S(2)}) collective-permute-start(f32[1,2048]{1,0:T(1,128)S(1)} %get-tuple-element.95), channel_id=1, source_target_pairs={{8,0},{9,1},{10,2},{11,3},{12,4},{13,5},{14,6},{15,7},{24,16},{25,... | collective-permute-start | bytes 24584 | tf_op jit(solution)/shard_map/ppermute | solution.py:43
  160.5 4.0 %collective-permute-start.19 = (f32[4,1,2048]{2,0,1:T(4,128)S(1)}, f32[4,1,2048]{2,0,1:T(4,128)S(1)}, u32[]{:S(2)}, u32[]{:S(2)}) collective-permute-start(f32[4,1,2048]{2,0,1:T(4,128)S(1)} %select_bitcast_fusion), channel_id=1, source_target_pairs={{0,4},{1,5},{2,6},{3,7},{4,0},{5,1},{6,2},{7,3},{8,12},{9,13},{10,... | collective-permute-start | bytes 98312 | tf_op jit(solution)/shard_map/ppermute | solution.py:33
  164.5 3.8 %collective-permute-start.20 = (f32[2,1,2048]{2,0,1:T(2,128)S(1)}, f32[2,1,2048]{2,0,1:T(2,128)S(1)}, u32[]{:S(2)}, u32[]{:S(2)}) collective-permute-start(f32[2,1,2048]{2,0,1:T(2,128)S(1)} %broadcast_select_fusion.4), channel_id=1, source_target_pairs={{0,2},{1,3},{2,0},{3,1},{4,6},{5,7},{6,4},{7,5},{8,10},{9,11},{10,... | collective-permute-start | bytes 49160 | tf_op jit(solution)/shard_map/ppermute | solution.py:33
  168.4 20.6 %collective-permute-start.21 = (f32[1,1,2048]{2,0,1:T(1,128)S(1)}, f32[1,1,2048]{2,0,1:T(1,128)S(1)}, u32[]{:S(2)}, u32[]{:S(2)}) collective-permute-start(f32[1,1,2048]{2,0,1:T(1,128)S(1)} %broadcast_select_fusion.5), channel_id=1, source_target_pairs={{0,1},{1,0},{2,3},{3,2},{4,5},{5,4},{6,7},{7,6},{8,9},{9,8},{10,11... | collective-permute-start | bytes 24584 | tf_op jit(solution)/shard_map/ppermute | solution.py:33
  (13 other events, 19.8 us)
